TPU v7x, 32 devices: a whole 2x2x4 slice. The times are simulated.
32 devices in a mesh: groups: 2 (over y), vocab: 4 (over z), tokens: 2 (over x), pair: 2 (over core).
Axes of the slice: x: 2, y: 2, z: 4, core: 2. Of those that a mesh axis runs over, the one named last changes fastest.
Arguments:
- hidden: bfloat16 [512, 5120], P(('groups', 'tokens'), 'pair'), parts along dimension 0, may hold values from -70 to 70
- student_head_weight: bfloat16 [5120, 5120], P('pair', ('vocab', 'tokens')), may hold values from -0.25 to 0.25
- down_weight: bfloat16 [2, 5120, 64], P('tokens', 'pair'), may hold values from -0.078125 to 0.078125
- up_weight: bfloat16 [2, 64, 5120], P(None, None, ('vocab', 'tokens')), may hold values from -0.75 to 0.75
- teacher: bfloat16 [512, 5120], P(('groups', 'pair'), ('vocab', 'tokens')), parts along dimension 0, may hold values from -25 to 260
- tenant: int32 [512], P('groups'), parts along dimension 0, may hold values from 0 to 1, as said below
- counted_row_mask: int32 [512], P(('groups', 'pair')), parts along dimension 0, may hold values 0 or 1
Outputs:
- token_kl: float32 [512], P(('groups', 'pair')), parts along dimension 0
- hidden_gradient: bfloat16 [512, 5120], P(('groups', 'vocab', 'tokens'), 'pair'), parts along dimension 0
- down_gradient: bfloat16 [4, 5120, 64], P(('groups', 'tokens'), 'pair'), parts along dimension 0
- up_gradient: bfloat16 [4, 64, 5120], P('groups', None, ('vocab', 'tokens')), parts along dimension 0
There are 2 independent parts, one for each index of `groups`. A program takes and returns all parts, laid end to end along the dimension named above; an argument that names none is the same for every part. Nothing has to cross between parts.
Inputs may be any that keep to these rules, and one draw needn't show every extreme that they name: Constant on aligned blocks of 64 rows; every tenant owns at least one block.
All inputs are finite; a program needn't handle non-finite values. No bound on the sum of `counted_row_mask` on one device may be relied on, other than what follows from the above.
Results may differ from a plain program's by a relative error of at most 0.009.
Values may be sent and summed in bfloat16 or wider, within the bound.
A program may use at most 64 MiB of HBM per device.

v0:
```python
import jax
import jax.numpy as jnp
from jax import lax
from jax.sharding import PartitionSpec as P

BLOCK = 64


ADAPTER_SCALE = 0.5


def shards(hidden, student_head_weight, down_weight, up_weight, teacher, tenant, counted_row_mask):
    all_rows = tenant.shape[0]
    half_rows = all_rows // lax.axis_size("pair")
    pair_index = lax.axis_index("pair")
    block_count = all_rows // BLOCK
    half_blocks = half_rows // BLOCK
    tenant_per_block = tenant.reshape(block_count, BLOCK)[:, 0]
    gathered = lax.all_gather(hidden, "tokens", axis=0, tiled=True)
    width = gathered.shape[1]
    adapter_rank = down_weight.shape[2]
    columns = student_head_weight.shape[1]
    tenant_number = up_weight.shape[0]
    owner_mask = tenant == lax.axis_index("tokens")
    lookup_tables = lax.all_gather(down_weight, "tokens", axis=0, tiled=True)
    selected_down = lookup_tables[tenant_per_block]
    partial_codes = jnp.einsum(
        "nmw,nwz->nmz",
        gathered.reshape(block_count, BLOCK, width),
        selected_down,
        preferred_element_type=jnp.float32,
    ).reshape(all_rows, adapter_rank)
    summed_codes = lax.psum(partial_codes, "pair")
    adapter_codes = summed_codes.astype(jnp.bfloat16)
    slab = gathered
    trunk_logits = lax.psum_scatter(
        jnp.dot(slab, student_head_weight, preferred_element_type=jnp.float32),
        "pair",
        scatter_dimension=0,
        tiled=True,
    )
    my_codes = lax.dynamic_slice_in_dim(adapter_codes, pair_index * half_rows, half_rows, 0)
    local_tenant = lax.dynamic_slice_in_dim(
        tenant_per_block, pair_index * half_blocks, half_blocks, 0
    )
    adapter_logits = jnp.einsum(
        "gji,giu->gju",
        my_codes.reshape(half_blocks, BLOCK, adapter_rank),
        up_weight[local_tenant],
        preferred_element_type=jnp.float32,
    ).reshape(half_rows, columns)
    student_model = trunk_logits + ADAPTER_SCALE * adapter_logits
    teacher_logits = teacher.astype(jnp.float32)
    peak_s, peak_t = lax.pmax(
        (jnp.max(student_model, axis=1), jnp.max(teacher_logits, axis=1)), ("vocab", "tokens")
    )
    exp_t = jnp.exp(teacher_logits - peak_t[:, None])
    sum_s, sum_t, cross_sum = lax.psum(
        (
            jnp.sum(jnp.exp(student_model - peak_s[:, None]), axis=1),
            jnp.sum(exp_t, axis=1),
            jnp.sum(exp_t * (teacher_logits - student_model), axis=1),
        ),
        ("vocab", "tokens"),
    )
    log_zs = peak_s + jnp.log(sum_s)
    log_zt = peak_t + jnp.log(sum_t)
    token_kl = cross_sum / sum_t - log_zt + log_zs
    weights = counted_row_mask.astype(jnp.float32) / all_rows
    grad_half = (
        weights[:, None]
        * (jnp.exp(student_model - log_zs[:, None]) - jnp.exp(teacher_logits - log_zt[:, None]))
    ).astype(jnp.bfloat16)
    full_grad = lax.all_gather(grad_half, "pair", axis=0, tiled=True)
    grad_blocks = full_grad.reshape(block_count, BLOCK, columns)
    selected_up = up_weight[tenant_per_block]
    code_part = jnp.einsum(
        "bkv,brv->bkr", grad_blocks, selected_up, preferred_element_type=jnp.float32
    ).reshape(all_rows, adapter_rank)
    code_gradient = lax.psum(code_part, ("vocab", "tokens")).astype(jnp.bfloat16)
    up_outer_product = jnp.einsum(
        "bkr,bkv->brv",
        adapter_codes.reshape(block_count, BLOCK, adapter_rank),
        grad_blocks,
        preferred_element_type=jnp.float32,
    )
    tenant_onehot = (tenant_per_block[:, None] == jnp.arange(tenant_number)[None, :]).astype(
        jnp.float32
    )
    up_gradient = (
        ADAPTER_SCALE
        * jnp.einsum(
            "yf,ysk->fsk", tenant_onehot, up_outer_product, precision=lax.Precision.HIGHEST
        )
    ).astype(jnp.bfloat16)
    owned_grad = jnp.where(owner_mask[:, None], code_gradient, jnp.zeros_like(code_gradient))
    down_gradient = (
        ADAPTER_SCALE
        * jnp.einsum("kd,kr->dr", gathered, owned_grad, preferred_element_type=jnp.float32)
    )[None].astype(jnp.bfloat16)
    shard_rows = all_rows // lax.axis_size(("vocab", "tokens"))
    slab = full_grad
    total = jnp.einsum("kv,dv->kd", slab, student_head_weight, preferred_element_type=jnp.float32)
    width_gradients = lax.psum_scatter(total, ("vocab", "tokens"), scatter_dimension=0, tiled=True)
    row_start = lax.axis_index(("vocab", "tokens")) * shard_rows
    my_grad_codes = lax.dynamic_slice_in_dim(code_gradient, row_start, shard_rows, 0)
    my_row_tenant = lax.dynamic_slice_in_dim(tenant, row_start, shard_rows, 0)
    width_gradients = width_gradients + ADAPTER_SCALE * jnp.einsum(
        "kr,kdr->kd",
        my_grad_codes,
        lookup_tables[my_row_tenant],
        preferred_element_type=jnp.float32,
    )
    hidden_gradient = width_gradients.astype(jnp.bfloat16)
    return (token_kl, hidden_gradient, down_gradient, up_gradient)


def solution(mesh):
    return jax.shard_map(
        shards,
        mesh=mesh,
        in_specs=(
            P(("groups", "tokens"), "pair"),
            P("pair", ("vocab", "tokens")),
            P("tokens", "pair", None),
            P(None, None, ("vocab", "tokens")),
            P(("groups", "pair"), ("vocab", "tokens")),
            P("groups"),
            P(("groups", "pair")),
        ),
        out_specs=(
            P(("groups", "pair")),
            P(("groups", "vocab", "tokens"), "pair"),
            P(("groups", "tokens"), "pair", None),
            P("groups", None, ("vocab", "tokens")),
        ),
        check_vma=False,
    )
```

profile of v0, /device:TPU:0, one launch (start us, length us, event | category | flops | bytes accessed | tf_op | source)
XLA Modules:
  0.0 194.5 jit_solution(1612701151491222273)
XLA Ops:
  7.2 0.0 copy-start
  7.2 0.0 all-gather.2.cloned.1.call-start
  7.2 0.7 all-gather.2.cloned.1.call-update
  7.9 0.0 reduce-scatter.3.cloned.1.call-start
  8.0 0.9 reshape.40
  8.9 1.5 reduce_max.23
  10.5 0.2 slice_reduce_fusion
  10.6 0.1 fusion.25
  10.7 25.8 %all-gather.2.cloned.1.call-done = bf16[256,2560]{1,0:T(8,128)(2,1)} async-done(((bf16[128,2560]{1,0:T(8,128)(2,1)}), bf16[256,2560]{1,0:T(8,128)(2,1)}) %all-gather.2.cloned.1.call-update) | async-done | bytes 1310736 | tf_op jit(solution)/shard_map/all_gather | solution.py:19
  36.5 0.0 copy-done
  36.5 3.4 %fusion.30 = f32[256,640]{1,0:T(8,128)} fusion(bf16[256,2560]{1,0:T(8,128)(2,1)} %all-gather.2.cloned.1.call-done, bf16[2560,640]{1,0:T(8,128)(2,1)S(1)} %copy-done), kind=kOutput, calls=%fused_computation.58 | convolution fusion | flops 838860800 | bytes 5242880 | tf_op jit(solution)/shard_map/dot_general | solution.py:37
  39.9 0.0 reduce-scatter.3.cloned.1.call-update
  39.9 0.0 reduce-scatter.5.cloned.1.call-start
  40.0 0.0 copy-done.3
  40.0 1.2 gather_fusion.1
  41.2 12.3 %all_gather.10 = bf16[2,2560,64]{1,2,0:T(8,128)(2,1)} all-gather(bf16[1,2560,64]{1,2,0:T(8,128)(2,1)} %param.9), channel_id=1, replica_groups=mesh['groups'=2,'vocab'=4,'tokens'=2,'pair'=2] {'tokens'}, dimensions={0}, use_global_device_ids=true | all-gather | bytes 983040 | tf_op jit(solution)/shard_map/all_gather | solution.py:25
  53.6 2.8 %gather_fusion = bf16[4,2560,64]{1,2,0:T(8,128)(2,1)} fusion(bf16[2,2560,64]{1,2,0:T(8,128)(2,1)} %all_gather.10, s32[1024]{0:T(1024)S(1)} %pad_clamp_fusion.2), kind=kCustom, calls=%fused_computation | custom fusion | bytes 2621456 | tf_op jit(solution)/shard_map/gather | solution.py:26
  56.4 0.6 convert_multiply_fusion
  57.0 2.2 %convolution_bitcast_fusion = f32[4,64,64]{1,2,0:T(8,128)S(1)} fusion(bf16[4,2560,64]{1,2,0:T(8,128)(2,1)} %gather_fusion, bf16[4,64,2560]{2,1,0:T(8,128)(2,1)} %bitcast.43), kind=kOutput, calls=%fused_computation.8 | convolution fusion | flops 83886080 | bytes 2686976 | tf_op jit(solution)/shard_map/nmw,nwz->nmz/dot_general | solution.py:27
  59.2 0.7 copy.24
  59.9 1.0 reshape.42
  61.0 3.6 %psum.35 = bf16[256,64]{0,1:T(8,128)(2,1)S(1)} all-reduce(f32[256,64]{0,1:T(8,128)S(1)} %reshape.42), channel_id=1, replica_groups=mesh['groups'=2,'vocab'=4,'tokens'=2,'pair'=2] {'pair'}, use_global_device_ids=true, to_apply=%region_3.0 | all-reduce | flops 16384 | bytes 98304 | tf_op jit(solution)/shard_map/psum | solution.py:33
  64.6 0.1 copy.25
  64.7 1.8 convolution_multiply_fusion.1
  66.5 1.8 fusion.29
  68.4 21.7 %all-reduce.2 = (f32[128]{0:T(128)S(1)}, f32[128]{0:T(128)S(1)}) all-reduce(f32[128]{0:T(128)S(1)} %get-tuple-element.15, bf16[128]{0:T(256)(128)(2,1)S(1)} %copy-done.7), channel_id=1, replica_groups=mesh['groups'=2,'vocab'=4,'tokens'=2,'pair'=2] {'vocab','tokens'}, use_global_device_ids=true, to_apply=%region_9.0 | all-reduce | flops 256 | bytes 1792 | tf_op jit(solution)/shard_map/pmax | solution.py:54
  90.0 1.8 fusion.7
  91.8 17.1 %all-reduce.1 = (f32[128]{0:T(128)S(1)}, f32[128]{0:T(128)S(1)}) all-reduce(f32[128]{0:T(128)S(1)} %get-tuple-element.5, f32[128]{0:T(128)S(1)} %get-tuple-element.6), channel_id=1, replica_groups=mesh['groups'=2,'vocab'=4,'tokens'=2,'pair'=2] {'vocab','tokens'}, use_global_device_ids=true, to_apply=%region_11.0 | all-reduce | flops 256 | bytes 2048 | tf_op jit(solution)/shard_map/psum | solution.py:58
  108.9 1.1 fusion.11
  110.1 2.0 %all_gather.11 = bf16[256,640]{1,0:T(8,128)(2,1)S(1)} all-gather(bf16[128,640]{1,0:T(8,128)(2,1)S(1)} %fusion.11), channel_id=1, replica_groups=mesh['groups'=2,'vocab'=4,'tokens'=2,'pair'=2] {'pair'}, dimensions={0}, use_global_device_ids=true | all-gather | bytes 491520 | tf_op jit(solution)/shard_map/all_gather | solution.py:74
  112.1 0.7 copy-done.1
  112.8 2.7 %fusion.31 = f32[256,2560]{1,0:T(8,128)} fusion(bf16[256,640]{1,0:T(8,128)(2,1)S(1)} %all_gather.11, bf16[2560,640]{1,0:T(8,128)(2,1)S(1)} %copy-done), kind=kOutput, calls=%fused_computation.59 | convolution fusion | flops 838860800 | bytes 6225920 | tf_op jit(solution)/shard_map/kv,dv->kd/dot_general | solution.py:103
  115.6 0.0 reduce-scatter.5.cloned.1.call-update
  115.6 0.9 copy-done.4
  116.5 1.3 gather_fusion.2
  117.8 0.1 compare_select_fusion.2
  117.9 6.8 %gather_fusion.3 = bf16[32,2560,64]{1,2,0:T(8,128)(2,1)} fusion(bf16[2,2560,64]{1,2,0:T(8,128)(2,1)} %all_gather.10, s32[1024]{0:T(1024)S(1)} %pad_clamp_fusion), kind=kCustom, calls=%fused_computation.3 | custom fusion | bytes 20971648 | tf_op jit(solution)/shard_map/gather | solution.py:111
  124.7 0.1 reshape.46
  124.8 1.3 fusion.32
  126.1 38.2 %all-reduce = (f32[128]{0:T(128)}, bf16[256,64]{1,0:T(8,128)(2,1)S(1)}) all-reduce(f32[128]{0:T(128)} %get-tuple-element.4, f32[256,64]{1,0:T(8,128)S(1)} %bitcast.44), channel_id=1, replica_groups=mesh['groups'=2,'vocab'=4,'tokens'=2,'pair'=2] {'vocab','tokens'}, use_global_device_ids=true, to_apply=%region_5.0 | all-reduce | flops 16512 | bytes 99328 | tf_op jit(solution)/shard_map/psum | solution.py:58
  164.3 2.5 %fusion.1 = bf16[1,2560,64]{1,2,0:T(8,128)(2,1)} fusion(bf16[256,2560]{1,0:T(8,128)(2,1)} %all-gather.2.cloned.1.call-done, bf16[256,64]{1,0:T(8,128)(2,1)S(1)} %get-tuple-element.10, pred[256]{0:T(512)(128)(4,1)S(1)} %broadcast_compare_fusion), kind=kOutput, calls=%fused_computation.6 | convolution fusion | flops 84230144 | bytes 1671424 | tf_op jit(solution)/shard_map/kd,kr->dr/dot_general | solution.py:99
  166.8 1.2 subtract_add_fusion
  168.0 1.2 fusion.15
  169.2 1.1 fusion.2
  170.3 0.7 fusion.14
  171.0 6.2 %fusion.20 = f32[32,1,2560]{2,1,0:T(1,128)} fusion(bf16[32,2560,64]{1,2,0:T(8,128)(2,1)} %gather_fusion.3, bf16[32,64,1]{1,0,2:T(8,128)(2,1)S(1)} %dynamic-slice_bitcast_fusion), kind=kOutput, calls=%fused_computation.34 | convolution fusion | flops 10485760 | bytes 10817536 | tf_op jit(solution)/shard_map/kr,kdr->kd/dot_general | solution.py:108
  177.2 8.9 %reduce-scatter.5.cloned.1.call-done = f32[32,2560]{1,0:T(8,128)} async-done(((f32[256,2560]{1,0:T(8,128)}), f32[32,2560]{1,0:T(8,128)}) %reduce-scatter.5.cloned.1.call-update) | async-done | bytes 327696 | tf_op jit(solution)/shard_map/reduce_scatter | solution.py:104
  186.2 1.8 fusion.13
  (21 shorter events, 0.1 us)
Async XLA Ops:
  7.2 29.4 %copy-start = (bf16[2560,640]{1,0:T(8,128)(2,1)S(1)}, bf16[2560,640]{1,0:T(8,128)(2,1)}, u32[]{:S(2)}) copy-start(bf16[2560,640]{1,0:T(8,128)(2,1)} %param.8) | copy-start | bytes 9830404
  7.2 29.4 %all-gather.2.cloned.1.call-start = ((), (), s32[]{:S(2)}) async-start(), calls=%async_computation.2 | async-start | bytes 1966080 | tf_op jit(solution)/shard_map/all_gather | solution.py:19
  7.9 58.6 %reduce-scatter.3.cloned.1.call-start = ((), (), s32[]{:S(2)}) async-start(), calls=%async_computation.3 | async-start | bytes 983040 | tf_op jit(solution)/shard_map/reduce_scatter | solution.py:36
  10.7 29.3 %copy-start.3 = (bf16[2,64,640]{2,1,0:T(8,128)(2,1)S(1)}, bf16[2,64,640]{2,1,0:T(8,128)(2,1)}, u32[]{:S(2)}) copy-start(bf16[2,64,640]{2,1,0:T(8,128)(2,1)} %param.10) | copy-start | bytes 491524
  39.9 146.2 %reduce-scatter.5.cloned.1.call-start = ((), (), s32[]{:S(2)}) async-start(), calls=%async_computation.4 | async-start | bytes 2949120 | tf_op jit(solution)/shard_map/reduce_scatter | solution.py:104
  53.6 2.8 %copy-start.8 = (s32[128]{0:T(128)S(1)}, s32[128]{0:T(128)}, u32[]{:S(2)}) copy-start(s32[128]{0:T(128)} %param.13) | copy-start | bytes 1540
  56.4 12.0 %copy-start.7 = (bf16[128]{0:T(256)(128)(2,1)S(1)}, bf16[128]{0:T(256)(128)(2,1)}, u32[]{:S(2)}) copy-start(bf16[128]{0:T(256)(128)(2,1)} %reduce_max.23) | copy-start | bytes 772
  56.4 33.6 %copy-start.2 = (bf16[128,640]{1,0:T(8,128)(2,1)S(1)}, bf16[128,640]{1,0:T(8,128)(2,1)}, u32[]{:S(2)}) copy-start(bf16[128,640]{1,0:T(8,128)(2,1)} %param.11) | copy-start | bytes 491524
  108.9 6.7 %copy-start.6 = (f32[128]{0:T(128)}, f32[128]{0:T(128)S(1)}, u32[]{:S(2)}) copy-start(f32[128]{0:T(128)S(1)} %get-tuple-element.12) | copy-start | bytes 1540
  112.1 0.7 copy-start.1
  115.6 0.9 copy-start.4
  115.6 2.2 %copy-start.5 = (s32[256]{0:T(256)S(1)}, s32[256]{0:T(256)}, u32[]{:S(2)}) copy-start(s32[256]{0:T(256)} %param.12) | copy-start | bytes 3076
Sparse Core Ops, SparseCore 0:
  9.6 26.9 all-gather.1
  40.1 8.0 reduce-scatter.2
  115.7 70.3 reduce-scatter.4
where the time goes:
time: 195 us; the launch traced here: 194 us
  blocking collectives  94.9 us (49%)
  waiting for transfers between devices  35.5 us (18%)
  matrix products  22.4 us (11%)
  local copies, waits for them, and re-layouts  16.7 us (9%)
  between operations  13.9 us (7%)
  other arithmetic  10.9 us (6%)
    psum x2, blocking collectives, shards(): lax.psum((jnp.sum(jnp.exp(student_model - peak_s[:, None]), axis=1), jnp....  55.3 us
    all_gather x1, waiting for transfers between devices, shards(): gathered = lax.all_gather(hidden, 'tokens', axis=0, tiled=True)  25.8 us
    pmax x1, blocking collectives, shards(): lax.pmax((jnp.max(student_model, axis=1), jnp.max(teacher_logits, axis=1)...  21.7 us
    all_gather x1, blocking collectives, shards(): lookup_tables = lax.all_gather(down_weight, 'tokens', axis=0, tiled=True)  12.3 us
    reduce_scatter x1, waiting for transfers between devices, shards(): lax.psum_scatter(total, ('vocab', 'tokens'), scatter_dimension=0, tiled=T...  8.95 us
    gather x1, local copies, waits for them, and re-layouts, shards(): lookup_tables[my_row_tenant]  6.79 us
    dot_general x1, matrix products, shards(): jnp.einsum('kr,kdr->kd', my_grad_codes, lookup_tables[my_row_tenant], pre...  6.22 us
  transfers between devices with their start and end apart: 3, of which 2 were waited for; matrix products, arithmetic and copies ran while one was open for 18% of the time, Pallas kernels for 0%

commit v1 on v0

--- a/solution.py
+++ b/solution.py
@@ -1,6 +1,10 @@
+import functools
+
 import jax
 import jax.numpy as jnp
 from jax import lax
+from jax.experimental import pallas as pl
+from jax.experimental.pallas import tpu as pltpu
 from jax.sharding import PartitionSpec as P
 
 BLOCK = 64
@@ -115,9 +119,307 @@
     return (token_kl, hidden_gradient, down_gradient, up_gradient)
 
 
+F32 = jnp.float32
+BF16 = jnp.bfloat16
+PARTS = 5
+NT = (((1,), (1,)), ((), ()))
+NN = (((1,), (0,)), ((), ()))
+
+
+def mm(a, b, dims=NN):
+    return lax.dot_general(a, b, dims, preferred_element_type=F32)
+
+
+def remote(src, dst, send, recv, where):
+    return pltpu.make_async_remote_copy(
+        src_ref=src, dst_ref=dst, send_sem=send, recv_sem=recv,
+        device_id=where, device_id_type=pl.DeviceIdType.MESH,
+    )
+
+
+def fused(
+    vocab_size, token_size,
+    hidden, weight, down_t, up, teacher, mask, counted,
+    kl_out, hidden_out, down_out, up_out,
+    h, w, d_dup, d_all, up_v, teach, acc, acc_in,
+    code_part, code_in, codes_mine, codes_other, codes_t,
+    stats, stats_in, flip, grad, cgp, cgp_in, cg_all, cg_t,
+    xs, xr, own, zs, zr,
+    lsem, hs, hr, pair_s, pair_r, tok_s, tok_r,
+    st_s, st_r, cp_s, cp_r, cg_s, cg_r, xs_s, xs_r, z_s, z_r,
+):
+    v, t, p = lax.axis_index("vocab"), lax.axis_index("tokens"), lax.axis_index("pair")
+    peers = vocab_size * token_size
+    me = v * token_size + t
+    mate = {"pair": 1 - p}
+    across = {"tokens": 1 - t}
+    rows, rank2 = mask.shape
+    half = rows // 2
+    rank = rank2 // 2
+    columns = weight.shape[1]
+    width = weight.shape[0]
+    part = width // PARTS
+    block = rows // peers
+
+    def peer(k):
+        b = lax.rem(me + k, peers)
+        return b, {"vocab": b // token_size, "tokens": lax.rem(b, token_size)}
+
+    def at_rows(i, n):
+        return pl.ds(pl.multiple_of(i * n, n), n)
+
+    local = [
+        pltpu.make_async_copy(hidden, h.at[at_rows(t, half)], lsem.at[0]),
+        pltpu.make_async_copy(weight, w, lsem.at[1]),
+        pltpu.make_async_copy(down_t, d_dup.at[pl.ds(0, rank)], lsem.at[2]),
+        pltpu.make_async_copy(down_t, d_dup.at[pl.ds(rank, rank)], lsem.at[3]),
+        pltpu.make_async_copy(down_t, d_all.at[at_rows(t, rank)], lsem.at[4]),
+        pltpu.make_async_copy(up, up_v, lsem.at[5]),
+        pltpu.make_async_copy(teacher, teach, lsem.at[6]),
+    ]
+    for copy in local:
+        copy.start()
+
+    barrier = pltpu.get_barrier_semaphore()
+    pl.semaphore_signal(barrier, inc=1, device_id=mate, device_id_type=pl.DeviceIdType.MESH)
+    for k in range(1, peers):
+        pl.semaphore_signal(barrier, inc=1, device_id=peer(k)[1], device_id_type=pl.DeviceIdType.MESH)
+    pl.semaphore_wait(barrier, peers)
+
+    quarter = half // 2
+    sends = []
+    for c in range(2):
+        sends.append(remote(
+            hidden.at[pl.ds(c * quarter, quarter)],
+            h.at[pl.ds(pl.multiple_of(t * half + c * quarter, quarter), quarter)],
+            hs.at[c], hr.at[c], across,
+        ))
+        sends[-1].start()
+    for copy in local:
+        copy.wait()
+
+    own_lane = (lax.broadcasted_iota(jnp.int32, (1, rank2), 1) // rank == t).astype(F32)
+
+    def forward(start, n):
+        sl = pl.ds(pl.multiple_of(start, n), n)
+        piece = h[sl, :]
+        code_part[sl, :] = mm(piece, d_dup[...], NT) * mask[sl, :] * own_lane
+        return sl, piece
+
+    sl, piece = forward(t * half, half)
+    acc[sl, :] = mm(piece, w[...])
+    for c in range(2):
+        sends[c].wait_recv()
+        sl, piece = forward((1 - t) * half + c * quarter, quarter)
+        if c == 1:
+            code_pair = remote(code_part, code_in, pair_s.at[0], pair_r.at[0], mate)
+            code_pair.start()
+        acc[sl, :] = mm(piece, w[...])
+    mate_rows = at_rows(1 - p, half)
+    my_rows = at_rows(p, half)
+    logit_pair = remote(acc.at[mate_rows], acc_in, pair_s.at[1], pair_r.at[1], mate)
+    logit_pair.start()
+    code_pair.wait_recv()
+    codes_mine[...] = (code_part[...] + code_in[...]).astype(BF16)
+    code_tok = remote(codes_mine, codes_other, tok_s.at[0], tok_r.at[0], across)
+    code_tok.start()
+
+    tl = teach[...].astype(F32)
+    peak_t = jnp.max(tl, axis=1, keepdims=True)
+    exp_t = jnp.exp(tl - peak_t)
+    sum_t = jnp.sum(exp_t, axis=1, keepdims=True)
+
+    logit_pair.wait_recv()
+    code_tok.wait_recv()
+    down_tok = remote(d_dup.at[pl.ds(0, rank)], d_all.at[at_rows(t, rank)], tok_s.at[1], tok_r.at[1], across)
+    codes = (codes_mine[...].astype(F32) + codes_other[...].astype(F32))
+    codes_mine_half = (codes_mine[my_rows, :].astype(F32) + codes_other[my_rows, :].astype(F32)).astype(BF16)
+    student = acc[my_rows, :] + acc_in[...] + ADAPTER_SCALE * mm(codes_mine_half, up_v[...])
+    peak_s = jnp.max(student, axis=1, keepdims=True)
+    sum_s = jnp.sum(jnp.exp(student - peak_s), axis=1, keepdims=True)
+    cross = jnp.sum(exp_t * (tl - student), axis=1, keepdims=True)
+
+    lane = lax.broadcasted_iota(jnp.int32, (half, 128), 1)
+    packed = jnp.zeros((half, 128), F32)
+    for i, value in enumerate((peak_s, sum_s, peak_t, sum_t, cross)):
+        packed = jnp.where(lane == i, value, packed)
+    stats[...] = packed.T[:8, :]
+    stat_sends = []
+    for k in range(1, peers):
+        stat_sends.append(remote(stats, stats_in.at[me], st_s.at[k], st_r.at[k], peer(k)[1]))
+        stat_sends[-1].start()
+    down_tok.start()
+    stats_in[me] = stats[...]
+    codes_t[...] = codes.T.astype(BF16)
+    for copy in stat_sends:
+        copy.wait_recv()
+    got = [stats_in[i] for i in range(peers)]
+    top_s, top_t = got[0][0:1], got[0][2:3]
+    for one in got[1:]:
+        top_s, top_t = jnp.maximum(top_s, one[0:1]), jnp.maximum(top_t, one[2:3])
+    zs_sum = zt_sum = cross_sum = jnp.zeros_like(top_s)
+    for one in got:
+        zs_sum = zs_sum + one[1:2] * jnp.exp(one[0:1] - top_s)
+        scale = jnp.exp(one[2:3] - top_t)
+        zt_sum = zt_sum + one[3:4] * scale
+        cross_sum = cross_sum + one[4:5] * scale
+    log_zs = top_s + jnp.log(zs_sum)
+    log_zt = top_t + jnp.log(zt_sum)
+    kl_out[...] = cross_sum / zt_sum - log_zt + log_zs
+    flip[...] = jnp.zeros_like(flip)
+    flip[0:1, :] = log_zs
+    flip[1:2, :] = log_zt
+    flip[2:3, :] = counted[...].astype(F32) / rows
+    cols = flip[...].T
+    grad_half = (cols[:, 2:3] * (jnp.exp(student - cols[:, 0:1]) - jnp.exp(tl - cols[:, 1:2]))).astype(BF16)
+    vh = vocab_size // 2
+    my_blocks = pl.ds(p * vh, vh)
+    grad[my_blocks] = grad_half.reshape(vh, token_size, block, columns)
+    grad_pair = remote(grad.at[my_blocks], grad.at[my_blocks], pair_s.at[2], pair_r.at[2], mate)
+    grad_pair.start()
+    grad_pair.wait_recv()
+
+    group = vocab_size * block
+    g_other = grad[:, 1 - t].reshape(group, columns)
+    x_sends = []
+    for j in range(PARTS):
+        xs[j] = mm(g_other, w[pl.ds(j * part, part), :], NT).astype(BF16).reshape(vocab_size, block, part)
+        x_sends.append(remote(xs.at[j], xr.at[j], xs_s.at[j], xs_r.at[j], across))
+        x_sends[-1].start()
+        if j == 0:
+            g_all = grad[...].reshape(rows, columns)
+            cgp[...] = (mm(g_all, up_v[...], NT) * mask[...]).astype(BF16).reshape(peers, block, rank2)
+            cp_sends = []
+            for k in range(1, peers):
+                b, where = peer(k)
+                cp_sends.append(remote(cgp.at[b], cgp_in.at[me], cp_s.at[k], cp_r.at[k], where))
+                cp_sends[-1].start()
+            cgp_in[me] = cgp[me]
+    g_own = grad[:, t].reshape(group, columns)
+    for j in range(PARTS):
+        own[j] = mm(g_own, w[pl.ds(j * part, part), :], NT).reshape(vocab_size, block, part)
+
+    for copy in cp_sends:
+        copy.wait_recv()
+    total = cgp_in[0].astype(F32)
+    for i in range(1, peers):
+        total = total + cgp_in[i].astype(F32)
+    cg_all[me] = total.astype(BF16)
+    cg_sends = []
+    for k in range(1, peers):
+        cg_sends.append(remote(cg_all.at[me], cg_all.at[me], cg_s.at[k], cg_r.at[k], peer(k)[1]))
+        cg_sends[-1].start()
+
+    up_out[...] = (ADAPTER_SCALE * mm(codes_t[...], g_all)).astype(BF16)
+
+    z_sends = []
+    for j in range(PARTS):
+        x_sends[j].wait_recv()
+        merged = own[j] + xr[j].astype(F32)
+        own[j] = merged
+        zs[j] = merged.astype(BF16)
+        for k in range(1, vocab_size):
+            to = lax.rem(v + k, vocab_size)
+            z_sends.append(remote(zs.at[j, to], zr.at[j, k], z_s.at[j, k], z_r.at[j, k], {"vocab": to}))
+            z_sends[-1].start()
+        if j == 0:
+            for copy in cg_sends:
+                copy.wait_recv()
+            cg_t[...] = cg_all[...].reshape(rows, rank2).astype(F32).T.astype(BF16)
+            mine = cg_t[at_rows(t, rank), :]
+        down_out[:, pl.ds(j * part, part)] = (ADAPTER_SCALE * mm(mine, h[:, pl.ds(j * part, part)])).astype(BF16)
+
+    down_tok.wait_recv()
+    my_cg = cg_all[me]
+    for j in range(PARTS):
+        for k in range(1, vocab_size):
+            z_sends[j * (vocab_size - 1) + k - 1].wait_recv()
+        value = own[j, v] + ADAPTER_SCALE * mm(my_cg, d_all[:, pl.ds(j * part, part)])
+        for k in range(1, vocab_size):
+            value = value + zr[j, k].astype(F32)
+        hidden_out[:, pl.ds(j * part, part)] = value.astype(BF16)
+
+    for copy in [code_pair, logit_pair, grad_pair, code_tok, down_tok] + sends + stat_sends + cp_sends + cg_sends + x_sends + z_sends:
+        copy.wait_send()
+
+
+def fused_shards(hidden, student_head_weight, down_weight, up_weight, teacher, tenant, counted_row_mask):
+    vocab_size, token_size = lax.axis_size("vocab"), lax.axis_size("tokens")
+    peers = vocab_size * token_size
+    rows = tenant.shape[0]
+    half = rows // 2
+    block = rows // peers
+    width, columns = student_head_weight.shape
+    tenants, rank, _ = up_weight.shape
+    rank2 = tenants * rank
+    part = width // PARTS
+    mask = (tenant[:, None] == (jnp.arange(rank2) // rank)[None, :]).astype(F32)
+    down_t = jnp.swapaxes(down_weight[0], 0, 1)
+    vmem = pl.BlockSpec(memory_space=pltpu.VMEM)
+    hbm = pl.BlockSpec(memory_space=pl.ANY)
+    dma = pltpu.SemaphoreType.DMA
+    kernel = functools.partial(fused, vocab_size, token_size)
+    token_kl, hidden_gradient, down_gradient, up_gradient = pl.pallas_call(
+        kernel,
+        out_shape=(
+            jax.ShapeDtypeStruct((1, half), F32),
+            jax.ShapeDtypeStruct((block, width), BF16),
+            jax.ShapeDtypeStruct((rank, width), BF16),
+            jax.ShapeDtypeStruct((rank2, columns), BF16),
+        ),
+        in_specs=[hbm] * 5 + [vmem] * 2,
+        out_specs=(vmem,) * 4,
+        scratch_shapes=[
+            pltpu.VMEM((rows, width), BF16),
+            pltpu.VMEM((width, columns), BF16),
+            pltpu.VMEM((rank2, width), BF16),
+            pltpu.VMEM((rank2, width), BF16),
+            pltpu.VMEM((rank2, columns), BF16),
+            pltpu.VMEM((half, columns), BF16),
+            pltpu.VMEM((rows, columns), F32),
+            pltpu.VMEM((half, columns), F32),
+            pltpu.VMEM((rows, rank2), F32),
+            pltpu.VMEM((rows, rank2), F32),
+            pltpu.VMEM((rows, rank2), BF16),
+            pltpu.VMEM((rows, rank2), BF16),
+            pltpu.VMEM((rank2, rows), BF16),
+            pltpu.VMEM((8, half), F32),
+            pltpu.VMEM((peers, 8, half), F32),
+            pltpu.VMEM((128, half), F32),
+            pltpu.VMEM((vocab_size, token_size, block, columns), BF16),
+            pltpu.VMEM((peers, block, rank2), BF16),
+            pltpu.VMEM((peers, block, rank2), BF16),
+            pltpu.VMEM((peers, block, rank2), BF16),
+            pltpu.VMEM((rank2, rows), BF16),
+            pltpu.VMEM((PARTS, vocab_size, block, part), BF16),
+            pltpu.VMEM((PARTS, vocab_size, block, part), BF16),
+            pltpu.VMEM((PARTS, vocab_size, block, part), F32),
+            pltpu.VMEM((PARTS, vocab_size, block, part), BF16),
+            pltpu.VMEM((PARTS, vocab_size, block, part), BF16),
+            dma((7,)), dma((2,)), dma((2,)), dma((3,)), dma((3,)), dma((2,)), dma((2,)),
+            dma((peers,)), dma((peers,)), dma((peers,)), dma((peers,)), dma((peers,)), dma((peers,)),
+            dma((PARTS,)), dma((PARTS,)), dma((PARTS, vocab_size)), dma((PARTS, vocab_size)),
+        ],
+        compiler_params=pltpu.CompilerParams(
+            collective_id=0, has_side_effects=True, vmem_limit_bytes=40 << 20
+        ),
+    )(hidden, student_head_weight, down_t, up_weight.reshape(rank2, columns), teacher, mask,
+      counted_row_mask.reshape(1, half))
+    return (
+        token_kl.reshape(half),
+        hidden_gradient,
+        jnp.swapaxes(down_gradient, 0, 1)[None],
+        up_gradient.reshape(tenants, rank, columns),
+    )
+
+
+def fits(mesh):
+    return mesh.shape["tokens"] == 2 and mesh.shape["vocab"] == 4
+
+
 def solution(mesh):
     return jax.shard_map(
-        shards,
+        fused_shards if fits(mesh) else shards,
         mesh=mesh,
         in_specs=(
             P(("groups", "tokens"), "pair"),

time: 195 us -> 77 us (0.39)
  blocking collectives: 94.9 us -> 0 us
  Pallas kernels: 0 us -> 66.2 us
  waiting for transfers between devices: 35.5 us -> 0 us
  matrix products: 22.4 us -> 0 us
  between operations: 13.9 us -> 0.67 us
  other arithmetic: 10.9 us -> 0.78 us
  local copies, waits for them, and re-layouts: 16.7 us -> 9.03 us
    pallas_call x0 -> x1, Pallas kernels: none -> 66.2 us  [fused_shards(): pl.pallas_call(kernel, out_shape=(jax.ShapeDtypeStruct((1, half), F32), j...]
    psum x3 -> x0, blocking collectives: 58.9 us -> none  [the longest x2 55.3 us: shards(): lax.psum((jnp.sum(jnp.exp(student_model - peak_s[:, None]), axis=1), jnp....]
    all_gather x1 -> x0, waiting for transfers between devices: 25.8 us -> none  [shards(): gathered = lax.all_gather(hidden, 'tokens', axis=0, tiled=True)]
    dot_general x9 -> x0, matrix products: 22.4 us -> none  [the longest x1 6.22 us: shards(): jnp.einsum('kr,kdr->kd', my_grad_codes, lookup_tables[my_row_tenant], pre...]
    pmax x1 -> x0, blocking collectives: 21.7 us -> none  [shards(): lax.pmax((jnp.max(student_model, axis=1), jnp.max(teacher_logits, axis=1)...]
    all_gather x2 -> x0, blocking collectives: 14.4 us -> none  [the longest x1 12.3 us: shards(): lookup_tables = lax.all_gather(down_weight, 'tokens', axis=0, tiled=True)]
    gather x4 -> x0, local copies, waits for them, and re-layouts: 12.1 us -> none  [the longest x1 6.79 us: shards(): lookup_tables[my_row_tenant]]
    reduce_scatter x2 -> x0, waiting for transfers between devices: 8.95 us -> none  [the longest x1 8.95 us: shards(): lax.psum_scatter(total, ('vocab', 'tokens'), scatter_dimension=0, tiled=T...]
  transfers between devices with their start and end apart: 3 -> 0, of which waited for: 2 -> 0; matrix products, arithmetic and copies ran while one was open for 18% -> 0% of each run, Pallas kernels for 0% -> 0%
where the time goes in v1:
time: 77 us; the launch traced here: 76.7 us
  Pallas kernels  66.2 us (86%)
  local copies, waits for them, and re-layouts  9.03 us (12%)
  other arithmetic  0.78 us (1%)
    pallas_call x1, Pallas kernels, fused_shards(): pl.pallas_call(kernel, out_shape=(jax.ShapeDtypeStruct((1, half), F32), j...  66.2 us
    unnamed x16, local copies, waits for them, and re-layouts  9.03 us

profile of v1, /device:TPU:0, one launch (start us, length us, event | category | flops | bytes accessed | tf_op | source)
XLA Modules:
  0.0 76.7 jit_solution(10578370645391561794)
XLA Ops:
  0.6 0.8 %compare_convert_fusion.mask = f32[256,128]{1,0:T(8,128)S(1)} fusion(s32[128]{0:T(128)S(1)} %and_select_fusion, s32[256]{0:T(256)} %param.12), kind=kLoop, calls=%fused_computation | loop fusion | flops 65536 | bytes 132608 | tf_op jit(solution)/shard_map/convert_element_type | solution.py:356
  1.4 0.0 copy-start
  1.4 1.9 %copy-done = bf16[2560,640]{1,0:T(8,128)(2,1)S(1)} copy-done((bf16[2560,640]{1,0:T(8,128)(2,1)S(1)}, bf16[2560,640]{1,0:T(8,128)(2,1)}, u32[]{:S(2)}) %copy-start) | copy-done | bytes 3276824
  3.4 0.0 copy-start.1
  3.4 1.1 %copy-done.1 = bf16[128,2560]{1,0:T(8,128)(2,1)S(1)} copy-done((bf16[128,2560]{1,0:T(8,128)(2,1)S(1)}, bf16[128,2560]{1,0:T(8,128)(2,1)}, u32[]{:S(2)}) %copy-start.1) | copy-done | bytes 655384
  4.4 0.0 copy-start.2
  4.4 1.0 %copy-done.2 = bf16[1,2560,64]{1,2,0:T(8,128)(2,1)S(1)} copy-done((bf16[1,2560,64]{1,2,0:T(8,128)(2,1)S(1)}, bf16[1,2560,64]{1,2,0:T(8,128)(2,1)}, u32[]{:S(2)}) %copy-start.2) | copy-done | bytes 327704
  5.4 0.0 copy-start.3
  5.4 0.9 %copy-done.3 = bf16[2,64,640]{2,1,0:T(8,128)(2,1)S(1)} copy-done((bf16[2,64,640]{2,1,0:T(8,128)(2,1)S(1)}, bf16[2,64,640]{2,1,0:T(8,128)(2,1)}, u32[]{:S(2)}) %copy-start.3) | copy-done | bytes 163864
  6.3 0.0 copy-start.4
  6.3 0.9 %copy-done.4 = bf16[128,640]{1,0:T(8,128)(2,1)S(1)} copy-done((bf16[128,640]{1,0:T(8,128)(2,1)S(1)}, bf16[128,640]{1,0:T(8,128)(2,1)}, u32[]{:S(2)}) %copy-start.4) | copy-done | bytes 163864
  7.2 0.0 copy-start.5
  7.3 0.7 copy-done.5
  7.9 66.2 %shard_map.102 = (f32[1,128]{1,0:T(1,128)S(1)}, bf16[32,2560]{1,0:T(8,128)(2,1)S(1)}, bf16[64,2560]{1,0:T(8,128)(2,1)S(1)}, bf16[128,640]{1,0:T(8,128)(2,1)S(1)}) custom-call(bf16[128,2560]{1,0:T(8,128)(2,1)S(1)} %copy-done.1, bf16[2560,640]{1,0:T(8,128)(2,1)S(1)} %copy-done, bf16[64,2560]{1,0:T(8,128)(2,1)S(1)} %bitcast.10, bf16[128,640]{1,0:T(8,128)(2,1)S(1)} %bitcast.12, ...), custom_call_target="tpu_custom_call" | custom-call | tf_op jit(solution)/shard_map/pallas_call | solution.py:362
  74.1 0.5 copy.15
  74.6 0.7 copy.16
  75.3 0.7 copy.17
  76.0 0.7 copy.18
  (1 shorter events, 0.0 us)
Async XLA Ops:
  1.4 1.9 %copy-start = (bf16[2560,640]{1,0:T(8,128)(2,1)S(1)}, bf16[2560,640]{1,0:T(8,128)(2,1)}, u32[]{:S(2)}) copy-start(bf16[2560,640]{1,0:T(8,128)(2,1)} %weight.1) | copy-start | bytes 9830404
  3.4 1.1 %copy-start.1 = (bf16[128,2560]{1,0:T(8,128)(2,1)S(1)}, bf16[128,2560]{1,0:T(8,128)(2,1)}, u32[]{:S(2)}) copy-start(bf16[128,2560]{1,0:T(8,128)(2,1)} %hidden.1) | copy-start | bytes 1966084
  4.4 1.0 %copy-start.2 = (bf16[1,2560,64]{1,2,0:T(8,128)(2,1)S(1)}, bf16[1,2560,64]{1,2,0:T(8,128)(2,1)}, u32[]{:S(2)}) copy-start(bf16[1,2560,64]{1,2,0:T(8,128)(2,1)} %param.9) | copy-start | bytes 983044
  5.4 0.9 %copy-start.3 = (bf16[2,64,640]{2,1,0:T(8,128)(2,1)S(1)}, bf16[2,64,640]{2,1,0:T(8,128)(2,1)}, u32[]{:S(2)}) copy-start(bf16[2,64,640]{2,1,0:T(8,128)(2,1)} %param.10) | copy-start | bytes 491524
  6.3 0.9 %copy-start.4 = (bf16[128,640]{1,0:T(8,128)(2,1)S(1)}, bf16[128,640]{1,0:T(8,128)(2,1)}, u32[]{:S(2)}) copy-start(bf16[128,640]{1,0:T(8,128)(2,1)} %teacher.1) | copy-start | bytes 491524
  7.2 0.7 copy-start.5

commit v2 on v1

--- a/solution.py
+++ b/solution.py
@@ -121,7 +121,8 @@
 
 F32 = jnp.float32
 BF16 = jnp.bfloat16
-PARTS = 5
+PARTS = 10
+PIECES = 4
 NT = (((1,), (1,)), ((), ()))
 NN = (((1,), (0,)), ((), ()))
 
@@ -145,8 +146,8 @@
     code_part, code_in, codes_mine, codes_other, codes_t,
     stats, stats_in, flip, grad, cgp, cgp_in, cg_all, cg_t,
     xs, xr, own, zs, zr,
-    lsem, hs, hr, pair_s, pair_r, tok_s, tok_r,
-    st_s, st_r, cp_s, cp_r, cg_s, cg_r, xs_s, xs_r, z_s, z_r,
+    lsem, hs, hr, fs, fr, pair_s, pair_r, tok_s, tok_r,
+    st_s, st_r, cp_s, cp_r, cg_s, cg_r, dn_s, dn_r, xs_s, xs_r, z_s, z_r,
 ):
     v, t, p = lax.axis_index("vocab"), lax.axis_index("tokens"), lax.axis_index("pair")
     peers = vocab_size * token_size
@@ -187,11 +188,15 @@
     pl.semaphore_wait(barrier, peers)
 
     quarter = half // 2
-    sends = []
-    for c in range(2):
+    piece_rows = quarter // PIECES
+    odd = lax.rem(v, 2)
+    neighbour = {"vocab": v + 1 - 2 * odd}
+    sends, forwards = [], []
+    for c in range(PIECES):
+        start = odd * quarter + c * piece_rows
         sends.append(remote(
-            hidden.at[pl.ds(c * quarter, quarter)],
-            h.at[pl.ds(pl.multiple_of(t * half + c * quarter, quarter), quarter)],
+            hidden.at[pl.ds(pl.multiple_of(start, piece_rows), piece_rows)],
+            h.at[pl.ds(pl.multiple_of(t * half + start, piece_rows), piece_rows)],
             hs.at[c], hr.at[c], across,
         ))
         sends[-1].start()
@@ -208,13 +213,20 @@
 
     sl, piece = forward(t * half, half)
     acc[sl, :] = mm(piece, w[...])
-    for c in range(2):
+    for c in range(PIECES):
         sends[c].wait_recv()
-        sl, piece = forward((1 - t) * half + c * quarter, quarter)
-        if c == 1:
-            code_pair = remote(code_part, code_in, pair_s.at[0], pair_r.at[0], mate)
-            code_pair.start()
-        acc[sl, :] = mm(piece, w[...])
+        start = pl.multiple_of((1 - t) * half + odd * quarter + c * piece_rows, piece_rows)
+        there = h.at[pl.ds(start, piece_rows)]
+        forwards.append(remote(there, there, fs.at[c], fr.at[c], neighbour))
+        forwards[-1].start()
+    sl, piece = forward((1 - t) * half + odd * quarter, quarter)
+    acc[sl, :] = mm(piece, w[...])
+    for copy in forwards:
+        copy.wait_recv()
+    sl, piece = forward((1 - t) * half + (1 - odd) * quarter, quarter)
+    code_pair = remote(code_part, code_in, pair_s.at[0], pair_r.at[0], mate)
+    code_pair.start()
+    acc[sl, :] = mm(piece, w[...])
     mate_rows = at_rows(1 - p, half)
     my_rows = at_rows(p, half)
     logit_pair = remote(acc.at[mate_rows], acc_in, pair_s.at[1], pair_r.at[1], mate)
@@ -223,6 +235,10 @@
     codes_mine[...] = (code_part[...] + code_in[...]).astype(BF16)
     code_tok = remote(codes_mine, codes_other, tok_s.at[0], tok_r.at[0], across)
     code_tok.start()
+    share = rank // vocab_size
+    sent = pl.ds(pl.multiple_of(t * rank + v * share, share), share)
+    down_tok = remote(d_dup.at[at_rows(v, share)], d_all.at[sent], tok_s.at[1], tok_r.at[1], across)
+    down_tok.start()
 
     tl = teach[...].astype(F32)
     peak_t = jnp.max(tl, axis=1, keepdims=True)
@@ -231,7 +247,6 @@
 
     logit_pair.wait_recv()
     code_tok.wait_recv()
-    down_tok = remote(d_dup.at[pl.ds(0, rank)], d_all.at[at_rows(t, rank)], tok_s.at[1], tok_r.at[1], across)
     codes = (codes_mine[...].astype(F32) + codes_other[...].astype(F32))
     codes_mine_half = (codes_mine[my_rows, :].astype(F32) + codes_other[my_rows, :].astype(F32)).astype(BF16)
     student = acc[my_rows, :] + acc_in[...] + ADAPTER_SCALE * mm(codes_mine_half, up_v[...])
@@ -248,7 +263,6 @@
     for k in range(1, peers):
         stat_sends.append(remote(stats, stats_in.at[me], st_s.at[k], st_r.at[k], peer(k)[1]))
         stat_sends[-1].start()
-    down_tok.start()
     stats_in[me] = stats[...]
     codes_t[...] = codes.T.astype(BF16)
     for copy in stat_sends:
@@ -277,6 +291,12 @@
     grad[my_blocks] = grad_half.reshape(vh, token_size, block, columns)
     grad_pair = remote(grad.at[my_blocks], grad.at[my_blocks], pair_s.at[2], pair_r.at[2], mate)
     grad_pair.start()
+    down_tok.wait_recv()
+    arrived = d_all.at[pl.ds(pl.multiple_of((1 - t) * rank + v * share, share), share)]
+    down_sends = []
+    for k in range(1, vocab_size):
+        down_sends.append(remote(arrived, arrived, dn_s.at[k], dn_r.at[k], {"vocab": lax.rem(v + k, vocab_size)}))
+        down_sends[-1].start()
     grad_pair.wait_recv()
 
     group = vocab_size * block
@@ -299,21 +319,21 @@
     for j in range(PARTS):
         own[j] = mm(g_own, w[pl.ds(j * part, part), :], NT).reshape(vocab_size, block, part)
 
-    for copy in cp_sends:
-        copy.wait_recv()
-    total = cgp_in[0].astype(F32)
-    for i in range(1, peers):
-        total = total + cgp_in[i].astype(F32)
-    cg_all[me] = total.astype(BF16)
-    cg_sends = []
-    for k in range(1, peers):
-        cg_sends.append(remote(cg_all.at[me], cg_all.at[me], cg_s.at[k], cg_r.at[k], peer(k)[1]))
-        cg_sends[-1].start()
-
     up_out[...] = (ADAPTER_SCALE * mm(codes_t[...], g_all)).astype(BF16)
 
     z_sends = []
     for j in range(PARTS):
+        if j == PARTS // 2:
+            for copy in cp_sends:
+                copy.wait_recv()
+            total = cgp_in[0].astype(F32)
+            for i in range(1, peers):
+                total = total + cgp_in[i].astype(F32)
+            cg_all[me] = total.astype(BF16)
+            cg_sends = []
+            for k in range(1, peers):
+                cg_sends.append(remote(cg_all.at[me], cg_all.at[me], cg_s.at[k], cg_r.at[k], peer(k)[1]))
+                cg_sends[-1].start()
         x_sends[j].wait_recv()
         merged = own[j] + xr[j].astype(F32)
         own[j] = merged
@@ -322,14 +342,13 @@
             to = lax.rem(v + k, vocab_size)
             z_sends.append(remote(zs.at[j, to], zr.at[j, k], z_s.at[j, k], z_r.at[j, k], {"vocab": to}))
             z_sends[-1].start()
-        if j == 0:
-            for copy in cg_sends:
-                copy.wait_recv()
-            cg_t[...] = cg_all[...].reshape(rows, rank2).astype(F32).T.astype(BF16)
-            mine = cg_t[at_rows(t, rank), :]
-        down_out[:, pl.ds(j * part, part)] = (ADAPTER_SCALE * mm(mine, h[:, pl.ds(j * part, part)])).astype(BF16)
-
-    down_tok.wait_recv()
+    for copy in cg_sends:
+        copy.wait_recv()
+    cg_t[...] = cg_all[...].reshape(rows, rank2).astype(F32).T.astype(BF16)
+    down_out[...] = (ADAPTER_SCALE * mm(cg_t[at_rows(t, rank), :], h[...])).astype(BF16)
+
+    for copy in down_sends:
+        copy.wait_recv()
     my_cg = cg_all[me]
     for j in range(PARTS):
         for k in range(1, vocab_size):
@@ -339,7 +358,7 @@
             value = value + zr[j, k].astype(F32)
         hidden_out[:, pl.ds(j * part, part)] = value.astype(BF16)
 
-    for copy in [code_pair, logit_pair, grad_pair, code_tok, down_tok] + sends + stat_sends + cp_sends + cg_sends + x_sends + z_sends:
+    for copy in [code_pair, logit_pair, grad_pair, code_tok, down_tok] + sends + forwards + down_sends + stat_sends + cp_sends + cg_sends + x_sends + z_sends:
         copy.wait_send()
 
 
@@ -396,12 +415,12 @@
             pltpu.VMEM((PARTS, vocab_size, block, part), F32),
             pltpu.VMEM((PARTS, vocab_size, block, part), BF16),
             pltpu.VMEM((PARTS, vocab_size, block, part), BF16),
-            dma((7,)), dma((2,)), dma((2,)), dma((3,)), dma((3,)), dma((2,)), dma((2,)),
+            dma((7,)), dma((PIECES,)), dma((PIECES,)), dma((PIECES,)), dma((PIECES,)), dma((3,)), dma((3,)), dma((2,)), dma((2,)),
             dma((peers,)), dma((peers,)), dma((peers,)), dma((peers,)), dma((peers,)), dma((peers,)),
-            dma((PARTS,)), dma((PARTS,)), dma((PARTS, vocab_size)), dma((PARTS, vocab_size)),
+            dma((vocab_size,)), dma((vocab_size,)), dma((PARTS,)), dma((PARTS,)), dma((PARTS, vocab_size)), dma((PARTS, vocab_size)),
         ],
         compiler_params=pltpu.CompilerParams(
-            collective_id=0, has_side_effects=True, vmem_limit_bytes=40 << 20
+            collective_id=0, has_side_effects=True, vmem_limit_bytes=60 << 20
         ),
     )(hidden, student_head_weight, down_t, up_weight.reshape(rank2, columns), teacher, mask,
       counted_row_mask.reshape(1, half))

time: 77 us -> 64.3 us (0.84)
  Pallas kernels: 66.2 us -> 55.9 us
  local copies, waits for them, and re-layouts: 9.03 us -> 6.07 us
    pallas_call x1, Pallas kernels: 66.2 us -> 55.9 us  [fused_shards(): pl.pallas_call(kernel, out_shape=(jax.ShapeDtypeStruct((1, half), F32), j...]
    unnamed x16 -> x4, local copies, waits for them, and re-layouts: 9.03 us -> 6.07 us
where the time goes in v2:
time: 64.3 us; the launch traced here: 64.1 us
  Pallas kernels  55.9 us (87%)
  local copies, waits for them, and re-layouts  6.07 us (9%)
  other arithmetic  1.44 us (2%)
  between operations  0.65 us (1%)
    pallas_call x1, Pallas kernels, fused_shards(): pl.pallas_call(kernel, out_shape=(jax.ShapeDtypeStruct((1, half), F32), j...  55.9 us
    unnamed x4, local copies, waits for them, and re-layouts  6.07 us
    convert_element_type x1, other arithmetic, fused_shards(): mask = (tenant[:, None] == (jnp.arange(rank2) // rank)[None, :]).astype(F32)  1.44 us

profile of v2, /device:TPU:0, one launch (start us, length us, event | category | flops | bytes accessed | tf_op | source)
XLA Modules:
  0.0 64.1 jit_solution(17601313417933135238)
XLA Ops:
  0.6 1.4 %compare_convert_fusion.mask = f32[256,128]{1,0:T(8,128)} fusion(s32[128]{0:T(128)S(1)} %and_select_fusion, s32[256]{0:T(256)} %param.12), kind=kLoop, calls=%fused_computation | loop fusion | flops 65536 | bytes 132608 | tf_op jit(solution)/shard_map/convert_element_type | solution.py:375
  2.1 55.9 %shard_map.102 = (f32[1,128]{1,0:T(1,128)}, bf16[32,2560]{1,0:T(8,128)(2,1)}, bf16[64,2560]{1,0:T(8,128)(2,1)}, bf16[128,640]{1,0:T(8,128)(2,1)}) custom-call(bf16[128,2560]{1,0:T(8,128)(2,1)} %hidden.1, bf16[2560,640]{1,0:T(8,128)(2,1)} %weight.1, bf16[64,2560]{1,0:T(8,128)(2,1)} %bitcast.10, bf16[128,640]{1,0:T(8,128)(2,1)} %bitcast.12, ...), custom_call_target="tpu_custom_call" | custom-call | tf_op jit(solution)/shard_map/pallas_call | solution.py:381
  58.0 1.2 %copy.15 = f32[128]{0:T(128)} copy(f32[128]{0:T(128)} %bitcast.15) | data formatting | bytes 1024
  59.2 1.6 %copy.16 = bf16[32,2560]{1,0:T(8,128)(2,1)} copy(bf16[32,2560]{1,0:T(8,128)(2,1)} %get-tuple-element.17) | data formatting | bytes 327680
  60.8 1.7 %copy.17 = bf16[1,2560,64]{1,2,0:T(8,128)(2,1)} copy(bf16[1,2560,64]{1,2,0:T(8,128)(2,1)} %bitcast.11) | data formatting | bytes 655360
  62.5 1.6 %copy.18 = bf16[2,64,640]{2,1,0:T(8,128)(2,1)} copy(bf16[2,64,640]{2,1,0:T(8,128)(2,1)} %bitcast.13) | data formatting | bytes 327680
  (1 shorter events, 0.0 us)

commit v3 on v2

--- a/solution.py
+++ b/solution.py
@@ -140,9 +140,9 @@
 
 def fused(
     vocab_size, token_size,
-    hidden, weight, down_t, up, teacher, mask, counted,
+    hidden, weight, down_t, up, teacher, tenant, counted,
     kl_out, hidden_out, down_out, up_out,
-    h, w, d_dup, d_all, up_v, teach, acc, acc_in,
+    mask, h, w, d_dup, d_all, up_v, teach, acc, acc_in,
     code_part, code_in, codes_mine, codes_other, codes_t,
     stats, stats_in, flip, grad, cgp, cgp_in, cg_all, cg_t,
     xs, xr, own, zs, zr,
@@ -200,6 +200,10 @@
             hs.at[c], hr.at[c], across,
         ))
         sends[-1].start()
+
+    tenant_of = lax.broadcasted_iota(jnp.int32, (rank2, rows), 0) // rank
+    mask[...] = (tenant_of == tenant[...]).astype(F32).T
+
     for copy in local:
         copy.wait()
 
@@ -233,8 +237,10 @@
     logit_pair.start()
     code_pair.wait_recv()
     codes_mine[...] = (code_part[...] + code_in[...]).astype(BF16)
-    code_tok = remote(codes_mine, codes_other, tok_s.at[0], tok_r.at[0], across)
+    code_tok = remote(codes_mine.at[my_rows], codes_other.at[my_rows], tok_s.at[0], tok_r.at[0], across)
     code_tok.start()
+    code_rest = remote(codes_mine.at[mate_rows], codes_other.at[mate_rows], tok_s.at[2], tok_r.at[2], across)
+    code_rest.start()
     share = rank // vocab_size
     sent = pl.ds(pl.multiple_of(t * rank + v * share, share), share)
     down_tok = remote(d_dup.at[at_rows(v, share)], d_all.at[sent], tok_s.at[1], tok_r.at[1], across)
@@ -247,7 +253,6 @@
 
     logit_pair.wait_recv()
     code_tok.wait_recv()
-    codes = (codes_mine[...].astype(F32) + codes_other[...].astype(F32))
     codes_mine_half = (codes_mine[my_rows, :].astype(F32) + codes_other[my_rows, :].astype(F32)).astype(BF16)
     student = acc[my_rows, :] + acc_in[...] + ADAPTER_SCALE * mm(codes_mine_half, up_v[...])
     peak_s = jnp.max(student, axis=1, keepdims=True)
@@ -264,7 +269,8 @@
         stat_sends.append(remote(stats, stats_in.at[me], st_s.at[k], st_r.at[k], peer(k)[1]))
         stat_sends[-1].start()
     stats_in[me] = stats[...]
-    codes_t[...] = codes.T.astype(BF16)
+    code_rest.wait_recv()
+    codes_t[...] = (codes_mine[...].astype(F32) + codes_other[...].astype(F32)).T.astype(BF16)
     for copy in stat_sends:
         copy.wait_recv()
     got = [stats_in[i] for i in range(peers)]
@@ -358,7 +364,7 @@
             value = value + zr[j, k].astype(F32)
         hidden_out[:, pl.ds(j * part, part)] = value.astype(BF16)
 
-    for copy in [code_pair, logit_pair, grad_pair, code_tok, down_tok] + sends + forwards + down_sends + stat_sends + cp_sends + cg_sends + x_sends + z_sends:
+    for copy in [code_pair, logit_pair, grad_pair, code_tok, code_rest, down_tok] + sends + forwards + down_sends + stat_sends + cp_sends + cg_sends + x_sends + z_sends:
         copy.wait_send()
 
 
@@ -372,7 +378,6 @@
     tenants, rank, _ = up_weight.shape
     rank2 = tenants * rank
     part = width // PARTS
-    mask = (tenant[:, None] == (jnp.arange(rank2) // rank)[None, :]).astype(F32)
     down_t = jnp.swapaxes(down_weight[0], 0, 1)
     vmem = pl.BlockSpec(memory_space=pltpu.VMEM)
     hbm = pl.BlockSpec(memory_space=pl.ANY)
@@ -389,6 +394,7 @@
         in_specs=[hbm] * 5 + [vmem] * 2,
         out_specs=(vmem,) * 4,
         scratch_shapes=[
+            pltpu.VMEM((rows, rank2), F32),
             pltpu.VMEM((rows, width), BF16),
             pltpu.VMEM((width, columns), BF16),
             pltpu.VMEM((rank2, width), BF16),
@@ -415,14 +421,14 @@
             pltpu.VMEM((PARTS, vocab_size, block, part), F32),
             pltpu.VMEM((PARTS, vocab_size, block, part), BF16),
             pltpu.VMEM((PARTS, vocab_size, block, part), BF16),
-            dma((7,)), dma((PIECES,)), dma((PIECES,)), dma((PIECES,)), dma((PIECES,)), dma((3,)), dma((3,)), dma((2,)), dma((2,)),
+            dma((7,)), dma((PIECES,)), dma((PIECES,)), dma((PIECES,)), dma((PIECES,)), dma((3,)), dma((3,)), dma((3,)), dma((3,)),
             dma((peers,)), dma((peers,)), dma((peers,)), dma((peers,)), dma((peers,)), dma((peers,)),
             dma((vocab_size,)), dma((vocab_size,)), dma((PARTS,)), dma((PARTS,)), dma((PARTS, vocab_size)), dma((PARTS, vocab_size)),
         ],
         compiler_params=pltpu.CompilerParams(
             collective_id=0, has_side_effects=True, vmem_limit_bytes=60 << 20
         ),
-    )(hidden, student_head_weight, down_t, up_weight.reshape(rank2, columns), teacher, mask,
+    )(hidden, student_head_weight, down_t, up_weight.reshape(rank2, columns), teacher, tenant.reshape(1, rows),
       counted_row_mask.reshape(1, half))
     return (
         token_kl.reshape(half),

time: 64.3 us -> 62 us (0.964)
  other arithmetic: 1.44 us -> 0 us
  Pallas kernels: 55.9 us -> 55.1 us
    convert_element_type x1 -> x0, other arithmetic: 1.44 us -> none  [fused_shards(): mask = (tenant[:, None] == (jnp.arange(rank2) // rank)[None, :]).astype(F32)]
    pallas_call x1, Pallas kernels: 55.9 us -> 55.1 us  [fused_shards(): pl.pallas_call(kernel, out_shape=(jax.ShapeDtypeStruct((1, half), F32), j...]
where the time goes in v3:
time: 62 us; the launch traced here: 61.8 us
  Pallas kernels  55.1 us (89%)
  local copies, waits for them, and re-layouts  6.07 us (10%)
  between operations  0.64 us (1%)
    pallas_call x1, Pallas kernels, fused_shards(): pl.pallas_call(kernel, out_shape=(jax.ShapeDtypeStruct((1, half), F32), j...  55.1 us
    unnamed x4, local copies, waits for them, and re-layouts  6.07 us

profile of v3, /device:TPU:0, one launch (start us, length us, event | category | flops | bytes accessed | tf_op | source)
XLA Modules:
  0.0 61.8 jit_solution(4413107025838086239)
XLA Ops:
  0.6 55.1 %shard_map.102 = (f32[1,128]{1,0:T(1,128)}, bf16[32,2560]{1,0:T(8,128)(2,1)}, bf16[64,2560]{1,0:T(8,128)(2,1)}, bf16[128,640]{1,0:T(8,128)(2,1)}) custom-call(bf16[128,2560]{1,0:T(8,128)(2,1)} %hidden.1, bf16[2560,640]{1,0:T(8,128)(2,1)} %weight.1, bf16[64,2560]{1,0:T(8,128)(2,1)} %bitcast.12, bf16[128,640]{1,0:T(8,128)(2,1)} %bitcast.14, ...), custom_call_target="tpu_custom_call" | custom-call | tf_op jit(solution)/shard_map/pallas_call | solution.py:386
  55.7 1.2 %copy.15 = f32[128]{0:T(128)} copy(f32[128]{0:T(128)} %bitcast.17) | data formatting | bytes 1024
  56.9 1.6 %copy.16 = bf16[32,2560]{1,0:T(8,128)(2,1)} copy(bf16[32,2560]{1,0:T(8,128)(2,1)} %get-tuple-element.17) | data formatting | bytes 327680
  58.5 1.7 %copy.17 = bf16[1,2560,64]{1,2,0:T(8,128)(2,1)} copy(bf16[1,2560,64]{1,2,0:T(8,128)(2,1)} %bitcast.11) | data formatting | bytes 655360
  60.2 1.6 %copy.18 = bf16[2,64,640]{2,1,0:T(8,128)(2,1)} copy(bf16[2,64,640]{2,1,0:T(8,128)(2,1)} %bitcast.13) | data formatting | bytes 327680

commit v4 on v3

--- a/solution.py
+++ b/solution.py
@@ -217,6 +217,13 @@
 
     sl, piece = forward(t * half, half)
     acc[sl, :] = mm(piece, w[...])
+    mate_rows = at_rows(1 - p, half)
+    my_rows = at_rows(p, half)
+
+    def logit_piece(q, i):
+        there = pl.ds(pl.multiple_of((1 - p) * half + q * quarter, quarter), quarter)
+        return remote(acc.at[there], acc_in.at[at_rows(q, quarter)], pair_s.at[i], pair_r.at[i], mate)
+
     for c in range(PIECES):
         sends[c].wait_recv()
         start = pl.multiple_of((1 - t) * half + odd * quarter + c * piece_rows, piece_rows)
@@ -225,16 +232,16 @@
         forwards[-1].start()
     sl, piece = forward((1 - t) * half + odd * quarter, quarter)
     acc[sl, :] = mm(piece, w[...])
+    logit_pair = logit_piece(odd, 1)
+    logit_pair.start()
     for copy in forwards:
         copy.wait_recv()
     sl, piece = forward((1 - t) * half + (1 - odd) * quarter, quarter)
     code_pair = remote(code_part, code_in, pair_s.at[0], pair_r.at[0], mate)
     code_pair.start()
     acc[sl, :] = mm(piece, w[...])
-    mate_rows = at_rows(1 - p, half)
-    my_rows = at_rows(p, half)
-    logit_pair = remote(acc.at[mate_rows], acc_in, pair_s.at[1], pair_r.at[1], mate)
-    logit_pair.start()
+    logit_last = logit_piece(1 - odd, 3)
+    logit_last.start()
     code_pair.wait_recv()
     codes_mine[...] = (code_part[...] + code_in[...]).astype(BF16)
     code_tok = remote(codes_mine.at[my_rows], codes_other.at[my_rows], tok_s.at[0], tok_r.at[0], across)
@@ -252,6 +259,7 @@
     sum_t = jnp.sum(exp_t, axis=1, keepdims=True)
 
     logit_pair.wait_recv()
+    logit_last.wait_recv()
     code_tok.wait_recv()
     codes_mine_half = (codes_mine[my_rows, :].astype(F32) + codes_other[my_rows, :].astype(F32)).astype(BF16)
     student = acc[my_rows, :] + acc_in[...] + ADAPTER_SCALE * mm(codes_mine_half, up_v[...])
@@ -364,8 +372,19 @@
             value = value + zr[j, k].astype(F32)
         hidden_out[:, pl.ds(j * part, part)] = value.astype(BF16)
 
-    for copy in [code_pair, logit_pair, grad_pair, code_tok, code_rest, down_tok] + sends + forwards + down_sends + stat_sends + cp_sends + cg_sends + x_sends + z_sends:
+    for copy in [code_pair, logit_pair, logit_last, grad_pair, code_tok, code_rest, down_tok] + sends + forwards + down_sends + stat_sends + cp_sends + cg_sends + x_sends + z_sends:
         copy.wait_send()
+
+
+def hand_over(a, b, c, d, a_out, b_out, c_out, d_out, sem):
+    copies = [
+        pltpu.make_async_copy(source, target, sem.at[i])
+        for i, (source, target) in enumerate(((a, a_out), (b, b_out), (c, c_out), (d, d_out)))
+    ]
+    for copy in copies:
+        copy.start()
+    for copy in copies:
+        copy.wait()
 
 
 def fused_shards(hidden, student_head_weight, down_weight, up_weight, teacher, tenant, counted_row_mask):
@@ -421,7 +440,7 @@
             pltpu.VMEM((PARTS, vocab_size, block, part), F32),
             pltpu.VMEM((PARTS, vocab_size, block, part), BF16),
             pltpu.VMEM((PARTS, vocab_size, block, part), BF16),
-            dma((7,)), dma((PIECES,)), dma((PIECES,)), dma((PIECES,)), dma((PIECES,)), dma((3,)), dma((3,)), dma((3,)), dma((3,)),
+            dma((7,)), dma((PIECES,)), dma((PIECES,)), dma((PIECES,)), dma((PIECES,)), dma((4,)), dma((4,)), dma((3,)), dma((3,)),
             dma((peers,)), dma((peers,)), dma((peers,)), dma((peers,)), dma((peers,)), dma((peers,)),
             dma((vocab_size,)), dma((vocab_size,)), dma((PARTS,)), dma((PARTS,)), dma((PARTS, vocab_size)), dma((PARTS, vocab_size)),
         ],
@@ -430,6 +449,15 @@
         ),
     )(hidden, student_head_weight, down_t, up_weight.reshape(rank2, columns), teacher, tenant.reshape(1, rows),
       counted_row_mask.reshape(1, half))
+    made = (token_kl, hidden_gradient, down_gradient, up_gradient)
+    token_kl, hidden_gradient, down_gradient, up_gradient = pl.pallas_call(
+        hand_over,
+        out_shape=tuple(jax.ShapeDtypeStruct(one.shape, one.dtype) for one in made),
+        in_specs=[hbm] * 4,
+        out_specs=(hbm,) * 4,
+        scratch_shapes=[dma((4,))],
+        compiler_params=pltpu.CompilerParams(vmem_limit_bytes=60 << 20),
+    )(*made)
     return (
         token_kl.reshape(half),
         hidden_gradient,

time: 62 us -> 76.9 us (1.24)
  Pallas kernels: 55.1 us -> 76.1 us
  local copies, waits for them, and re-layouts: 6.07 us -> 0 us
    pallas_call x0 -> x1, Pallas kernels: none -> 21 us  [fused_shards(): pl.pallas_call(hand_over, out_shape=tuple((jax.ShapeDtypeStruct(one.shape...]
    unnamed x4 -> x0, local copies, waits for them, and re-layouts: 6.07 us -> none
where the time goes in v4:
time: 76.9 us; the launch traced here: 76.7 us
  Pallas kernels  76.1 us (99%)
    pallas_call x1, Pallas kernels, fused_shards(): pl.pallas_call(kernel, out_shape=(jax.ShapeDtypeStruct((1, half), F32), j...  55.1 us
    pallas_call x1, Pallas kernels, fused_shards(): pl.pallas_call(hand_over, out_shape=tuple((jax.ShapeDtypeStruct(one.shape...  21 us

profile of v4, /device:TPU:0, one launch (start us, length us, event | category | flops | bytes accessed | tf_op | source)
XLA Modules:
  0.0 76.7 jit_solution(2605880303860528851)
XLA Ops:
  0.6 55.1 %shard_map.102 = (f32[1,128]{1,0:T(1,128)}, bf16[32,2560]{1,0:T(8,128)(2,1)}, bf16[64,2560]{1,0:T(8,128)(2,1)}, bf16[128,640]{1,0:T(8,128)(2,1)}) custom-call(bf16[128,2560]{1,0:T(8,128)(2,1)} %hidden.1, bf16[2560,640]{1,0:T(8,128)(2,1)} %weight.1, bf16[64,2560]{1,0:T(8,128)(2,1)} %bitcast.11, bf16[128,640]{1,0:T(8,128)(2,1)} %bitcast.12, ...), custom_call_target="tpu_custom_call" | custom-call | tf_op jit(solution)/shard_map/pallas_call | solution.py:405
  55.7 21.0 %shard_map.103 = (f32[1,128]{1,0:T(1,128)}, bf16[32,2560]{1,0:T(8,128)(2,1)}, bf16[64,2560]{1,0:T(8,128)(2,1)}, bf16[128,640]{1,0:T(8,128)(2,1)}) custom-call(f32[1,128]{1,0:T(1,128)} %get-tuple-element.12.a, bf16[32,2560]{1,0:T(8,128)(2,1)} %get-tuple-element.13.b, bf16[64,2560]{1,0:T(8,128)(2,1)} %get-tuple-element.14.c, bf16[128,640]{1,0:T(8,128)(2,1)} %get-tuple-element.15.d), custom_call_target="tpu_custom_call" | custom-call | tf_op jit(solution)/shard_map/pallas_call | solution.py:453

commit v5 on v4

--- a/solution.py
+++ b/solution.py
@@ -376,15 +376,17 @@
         copy.wait_send()
 
 
-def hand_over(a, b, c, d, a_out, b_out, c_out, d_out, sem):
-    copies = [
-        pltpu.make_async_copy(source, target, sem.at[i])
-        for i, (source, target) in enumerate(((a, a_out), (b, b_out), (c, c_out), (d, d_out)))
-    ]
-    for copy in copies:
-        copy.start()
-    for copy in copies:
-        copy.wait()
+def hand_over(*refs):
+    sources, targets, held, sem_in, sem_out = refs[:4], refs[4:8], refs[8:12], refs[12], refs[13]
+    reads = [pltpu.make_async_copy(sources[i], held[i], sem_in.at[i]) for i in range(4)]
+    writes = [pltpu.make_async_copy(held[i], targets[i], sem_out.at[i]) for i in range(4)]
+    for read in reads:
+        read.start()
+    for read, write in zip(reads, writes):
+        read.wait()
+        write.start()
+    for write in writes:
+        write.wait()
 
 
 def fused_shards(hidden, student_head_weight, down_weight, up_weight, teacher, tenant, counted_row_mask):
@@ -455,7 +457,7 @@
         out_shape=tuple(jax.ShapeDtypeStruct(one.shape, one.dtype) for one in made),
         in_specs=[hbm] * 4,
         out_specs=(hbm,) * 4,
-        scratch_shapes=[dma((4,))],
+        scratch_shapes=[pltpu.VMEM(one.shape, one.dtype) for one in made] + [dma((4,)), dma((4,))],
         compiler_params=pltpu.CompilerParams(vmem_limit_bytes=60 << 20),
     )(*made)
     return (

time: 76.9 us -> 57.8 us (0.75)
  Pallas kernels: 76.1 us -> 57 us
    pallas_call x1, Pallas kernels: 21 us -> 1.91 us  [fused_shards(): pl.pallas_call(hand_over, out_shape=tuple((jax.ShapeDtypeStruct(one.shape...]
where the time goes in v5:
time: 57.8 us; the launch traced here: 57.6 us
  Pallas kernels  57 us (99%)
  between operations  0.64 us (1%)
    pallas_call x1, Pallas kernels, fused_shards(): pl.pallas_call(kernel, out_shape=(jax.ShapeDtypeStruct((1, half), F32), j...  55.1 us
    pallas_call x1, Pallas kernels, fused_shards(): pl.pallas_call(hand_over, out_shape=tuple((jax.ShapeDtypeStruct(one.shape...  1.91 us

profile of v5, /device:TPU:0, one launch (start us, length us, event | category | flops | bytes accessed | tf_op | source)
XLA Modules:
  0.0 57.6 jit_solution(10616222499097891427)
XLA Ops:
  0.6 55.1 %shard_map.102 = (f32[1,128]{1,0:T(1,128)}, bf16[32,2560]{1,0:T(8,128)(2,1)}, bf16[64,2560]{1,0:T(8,128)(2,1)}, bf16[128,640]{1,0:T(8,128)(2,1)}) custom-call(bf16[128,2560]{1,0:T(8,128)(2,1)} %hidden.1, bf16[2560,640]{1,0:T(8,128)(2,1)} %weight.1, bf16[64,2560]{1,0:T(8,128)(2,1)} %bitcast.11, bf16[128,640]{1,0:T(8,128)(2,1)} %bitcast.12, ...), custom_call_target="tpu_custom_call" | custom-call | tf_op jit(solution)/shard_map/pallas_call | solution.py:407
  55.7 1.9 %shard_map.103 = (f32[1,128]{1,0:T(1,128)}, bf16[32,2560]{1,0:T(8,128)(2,1)}, bf16[64,2560]{1,0:T(8,128)(2,1)}, bf16[128,640]{1,0:T(8,128)(2,1)}) custom-call(f32[1,128]{1,0:T(1,128)} %get-tuple-element.12.refs_0_, bf16[32,2560]{1,0:T(8,128)(2,1)} %get-tuple-element.13.refs_1_, bf16[64,2560]{1,0:T(8,128)(2,1)} %get-tuple-element.14.refs_2_, ...), custom_call_target="tpu_custom_call" | custom-call | tf_op jit(solution)/shard_map/pallas_call | solution.py:455
